TPU v7x, 128 devices: a whole 4x4x4 slice. The times are simulated.
128 devices in a mesh: tok: 128 (over y, z, x, core).
Axes of the slice: x: 4, y: 4, z: 4, core: 2. Of those that a mesh axis runs over, the one named last changes fastest.
Arguments:
- activations: bfloat16 [360448, 4096], P('tok'), may hold values from -70 to 70
- sketch: bfloat16 [4096, 128], replicated, may hold values from -0.09375 to 0.09375
Outputs:
- projection: float32 [4096, 128], replicated
All inputs are finite; a program needn't handle non-finite values.
Results may differ from a plain program's by a relative error of at most 0.0003.
Values sent between devices are 32-bit elements; how exact they have to be, the bound alone decides.
A program may use at most 128 MiB of HBM per device.

v0:
```python
import jax
import jax.numpy as jnp
from jax import lax
from jax.sharding import PartitionSpec as P


def partner_2(block, axis, bit):
    count = lax.axis_size(axis)
    route = []
    for low in range(count):
        high = low | 1 << bit
        if high != low and high < count:
            route += [(low, high), (high, low)]
    return lax.ppermute(block, axis, route)


def upper_cholesky(gram):
    width = gram.shape[0]
    places = jnp.arange(width)

    def column_step(step, carry):
        remain, upper = carry
        row = lax.dynamic_slice_in_dim(remain, step, 1, 0)[0]
        pivot = jnp.sqrt(jnp.sum(jnp.where(places == step, row, 0.0)))
        scaled = jnp.where(places >= step, row / pivot, 0.0)
        upper = upper + jnp.where((places == step)[:, None], scaled[None, :], 0.0)
        remain = remain - scaled[:, None] * scaled[None, :]
        return (remain, upper)

    start = (gram, jnp.zeros_like(gram))
    _, upper = lax.fori_loop(0, width, column_step, start)
    return upper


def upper_inverse(upper):
    width = upper.shape[0]
    places = jnp.arange(width)

    def row_step(count, inverse):
        index = width - 1 - count
        row = lax.dynamic_slice_in_dim(upper, index, 1, 0)[0]
        diag_value = jnp.sum(jnp.where(places == index, row, 0.0))
        beyond = jnp.where(places > index, row, 0.0)
        known = jnp.dot(beyond, inverse, precision=lax.Precision.HIGHEST)
        unit = jnp.where(places == index, 1.0, 0.0)
        fresh = (unit - known) / diag_value
        return inverse + jnp.where((places == index)[:, None], fresh[None, :], 0.0)

    return lax.fori_loop(0, width, row_step, jnp.zeros_like(upper))


def apply_inverse(matrix, factor):
    return jnp.dot(matrix, upper_inverse(factor), precision=lax.Precision.HIGHEST)


def merge_factors(lower_part, upper_part):
    first_gram = lax.dot_general(
        lower_part, lower_part, (((0,), (0,)), ((), ())), precision=lax.Precision.HIGHEST
    )
    second_gram = lax.dot_general(
        upper_part, upper_part, (((0,), (0,)), ((), ())), precision=lax.Precision.HIGHEST
    )
    return upper_cholesky(first_gram + second_gram)


def local(activations, sketch):
    sampled = jnp.dot(activations, sketch, preferred_element_type=jnp.float32)
    sampled_low = sampled.astype(jnp.bfloat16)
    local_partial = lax.dot_general(
        activations, sampled_low, (((0,), (0,)), ((), ())), preferred_element_type=jnp.float32
    )
    local_gram = lax.dot_general(
        sampled, sampled, (((0,), (0,)), ((), ())), precision=lax.Precision.HIGHEST
    )
    factor = upper_cholesky(local_gram)
    levels = lax.axis_size("tok").bit_length() - 1
    for level in range(levels):
        partner = partner_2(factor, "tok", level)
        is_lower = lax.axis_index("tok") >> level & 1 == 0
        first_block = jnp.where(is_lower, factor, partner)
        second_block = jnp.where(is_lower, partner, factor)
        factor = merge_factors(first_block, second_block)
    term = apply_inverse(local_partial, factor)
    return lax.psum(term, "tok")


def solution(mesh):
    placed = (P("tok", None), P())
    return jax.shard_map(local, mesh=mesh, in_specs=placed, out_specs=P(), check_vma=False)
```

profile of v0, /device:TPU:1, one launch (start us, length us, event | category | flops | bytes accessed | tf_op | source)
XLA Modules:
  0.0 2047.4 jit_solution(729694027582978735)
XLA Ops:
  6.5 1.2 copy-done
  7.8 10.7 fusion.83
  18.5 2.4 fusion.84
  20.9 206.8 %while.153 = (s32[]{:T(128)}, f32[128,128]{1,0:T(8,128)S(1)}, f32[128,128]{1,0:T(8,128)S(1)}, s32[]{:T(128)}, s32[]{:T(128)}) while((s32[]{:T(128)}, f32[128,128]{1,0:T(8,128)S(1)}, f32[128,128]{1,0:T(8,128)S(1)}, s32[]{:T(128)}, s32[]{:T(128)}) %tuple.307), condition=%wide.region_2.3_spmd.clone.clone, body=%wide.region_0.2_spmd.clone.clone.sunk | while | flops 83202 | bytes 270175 | solution.py:31
  227.7 1.5 collective-permute-start
  229.2 0.9 collective-permute-done
  230.7 206.8 %while.154 = (s32[]{:T(128)}, f32[128,128]{1,0:T(8,128)S(1)}, f32[128,128]{1,0:T(8,128)S(1)}, s32[]{:T(128)}, s32[]{:T(128)}) while((s32[]{:T(128)}, f32[128,128]{1,0:T(8,128)S(1)}, f32[128,128]{1,0:T(8,128)S(1)}, s32[]{:T(128)}, s32[]{:T(128)}) %tuple.310), condition=%wide.region_5.6_spmd.clone.clone, body=%wide.region_3.5_spmd.clone.clone.sunk | while | flops 83202 | bytes 270175 | solution.py:31
  437.4 1.4 collective-permute-start.1
  438.8 1.8 collective-permute-done.1
  441.2 206.8 %while.155 = (s32[]{:T(128)}, f32[128,128]{1,0:T(8,128)S(1)}, f32[128,128]{1,0:T(8,128)S(1)}, s32[]{:T(128)}, s32[]{:T(128)}) while((s32[]{:T(128)}, f32[128,128]{1,0:T(8,128)S(1)}, f32[128,128]{1,0:T(8,128)S(1)}, s32[]{:T(128)}, s32[]{:T(128)}) %tuple.313), condition=%wide.region_8.9_spmd.clone.clone, body=%wide.region_6.8_spmd.clone.clone.sunk | while | flops 83202 | bytes 270175 | solution.py:31
  648.0 2.9 collective-permute-start.2
  650.9 1.8 collective-permute-done.2
  653.3 206.8 %while.156 = (s32[]{:T(128)}, f32[128,128]{1,0:T(8,128)S(1)}, f32[128,128]{1,0:T(8,128)S(1)}, s32[]{:T(128)}, s32[]{:T(128)}) while((s32[]{:T(128)}, f32[128,128]{1,0:T(8,128)S(1)}, f32[128,128]{1,0:T(8,128)S(1)}, s32[]{:T(128)}, s32[]{:T(128)}) %tuple.316), condition=%wide.region_11.12_spmd.clone.clone, body=%wide.region_9.11_spmd.clone.clone.sunk | while | flops 83202 | bytes 270175 | solution.py:31
  860.0 1.8 collective-permute-start.3
  861.8 1.7 collective-permute-done.3
  864.1 206.8 %while.157 = (s32[]{:T(128)}, f32[128,128]{1,0:T(8,128)S(1)}, f32[128,128]{1,0:T(8,128)S(1)}, s32[]{:T(128)}, s32[]{:T(128)}) while((s32[]{:T(128)}, f32[128,128]{1,0:T(8,128)S(1)}, f32[128,128]{1,0:T(8,128)S(1)}, s32[]{:T(128)}, s32[]{:T(128)}) %tuple.319), condition=%wide.region_14.15_spmd.clone.clone, body=%wide.region_12.14_spmd.clone.clone.sunk | while | flops 83202 | bytes 270175 | solution.py:31
  1070.8 3.5 collective-permute-start.4
  1074.3 1.7 collective-permute-done.4
  1076.6 206.8 %while.158 = (s32[]{:T(128)}, f32[128,128]{1,0:T(8,128)S(1)}, f32[128,128]{1,0:T(8,128)S(1)}, s32[]{:T(128)}, s32[]{:T(128)}) while((s32[]{:T(128)}, f32[128,128]{1,0:T(8,128)S(1)}, f32[128,128]{1,0:T(8,128)S(1)}, s32[]{:T(128)}, s32[]{:T(128)}) %tuple.322), condition=%wide.region_17.18_spmd.clone.clone, body=%wide.region_15.17_spmd.clone.clone.sunk | while | flops 83202 | bytes 270175 | solution.py:31
  1283.3 1.4 collective-permute-start.5
  1284.7 1.8 collective-permute-done.5
  1287.1 206.8 %while.159 = (s32[]{:T(128)}, f32[128,128]{1,0:T(8,128)S(1)}, f32[128,128]{1,0:T(8,128)S(1)}, s32[]{:T(128)}, s32[]{:T(128)}) while((s32[]{:T(128)}, f32[128,128]{1,0:T(8,128)S(1)}, f32[128,128]{1,0:T(8,128)S(1)}, s32[]{:T(128)}, s32[]{:T(128)}) %tuple.325), condition=%wide.region_20.21_spmd.clone.clone, body=%wide.region_18.20_spmd.clone.clone.sunk | while | flops 83202 | bytes 270175 | solution.py:31
  1493.9 3.2 collective-permute-start.6
  1497.1 12.1 fusion.46
  1509.7 178.9 %while.160 = (s32[]{:T(128)}, f32[128,128]{1,0:T(8,128)S(1)}, f32[128,128]{1,0:T(8,128)S(1)}, s32[]{:T(128)}, s32[]{:T(128)}) while((s32[]{:T(128)}, f32[128,128]{1,0:T(8,128)S(1)}, f32[128,128]{1,0:T(8,128)S(1)}, s32[]{:T(128)}, s32[]{:T(128)}) %tuple.328), condition=%wide.region_23.24_spmd.clone.clone, body=%wide.region_21.23_spmd.clone.clone.sunk | while | flops 83202 | bytes 270175 | solution.py:31
  1688.6 186.7 %while.161 = (s32[]{:T(128)}, f32[128,128]{1,0:T(8,128)S(1)}, f32[128,128]{1,0:T(8,128)S(1)}, s32[]{:T(128)}, s32[]{:T(128)}, /*index=5*/s32[]{:T(128)}, s32[]{:T(128)}) while((s32[]{:T(128)}, f32[128,128]{1,0:T(8,128)S(1)}, f32[128,128]{1,0:T(8,128)S(1)}, s32[]{:T(128)}, s32[]{:T(128)}, /*index=5*/s32[]{:T(128)}, ...), condition=%wide.region_26.27_spmd.clone.clone, body=%wide.region_24.26_spmd.clone.clone.sunk | while | flops 263430 | bytes 201121 | solution.py:49
  1692.2 0.7 fusion.132
  1699.5 0.7 fusion.132
  1703.9 0.7 fusion.132
  1711.1 0.7 fusion.132
  1715.5 0.7 fusion.132
  1719.9 0.7 fusion.132
  1727.2 0.7 fusion.132
  1731.6 0.7 fusion.132
  1738.9 0.7 fusion.132
  1743.2 0.7 fusion.132
  1747.6 0.7 fusion.132
  1754.9 0.7 fusion.132
  1759.3 0.7 fusion.132
  1766.6 0.7 fusion.132
  1771.0 0.7 fusion.132
  1775.3 0.7 fusion.132
  1782.6 0.7 fusion.132
  1787.0 0.7 fusion.132
  1794.3 0.7 fusion.132
  1875.4 6.3 fusion.85
  1881.7 155.8 %all-reduce.2.cloned.1.call-done = f32[4096,128]{1,0:T(8,128)} async-done(((f32[4096,128]{1,0:T(8,128)}), f32[4096,128]{1,0:T(8,128)}) %all-reduce.2.cloned.1.call-update) | async-done | bytes 2097168 | tf_op jit(solution)/shard_map/psum | solution.py:84
  2037.5 3.0 copy.82
  (5640 shorter events, 1013.7 us)
Async XLA Ops:
  6.5 1.2 copy-start
  6.5 2031.0 %all-reduce.2.cloned.1.call-start = ((), (), s32[]{:S(2)}) async-start(), calls=%async_computation | async-start | bytes 4194304 | tf_op jit(solution)/shard_map/psum | solution.py:84
  227.7 2.4 collective-permute-start
  437.4 3.2 collective-permute-start.1
  648.0 4.7 collective-permute-start.2
  860.0 3.5 collective-permute-start.3
  1070.8 5.2 collective-permute-start.4
  1283.3 3.2 collective-permute-start.5
  1493.9 15.2 collective-permute-start.6
Sparse Core Ops, SparseCore 0:
  1881.9 155.5 all-reduce.1
where the time goes:
time: 2060 us; the launch traced here: 2050 us
  other arithmetic  932 us (45%)
  loops' own time  790 us (38%)
  waiting for transfers between devices  165 us (8%)
  matrix products  127 us (6%)
    another operation x8, loops' own time, upper_cholesky(): _, upper = lax.fori_loop(0, width, column_step, start)  785 us
    reduce_sum x1024, other arithmetic, column_step(): pivot = jnp.sqrt(jnp.sum(jnp.where(places == step, row, 0.0)))  692 us
    psum x1, waiting for transfers between devices, local(): return lax.psum(term, 'tok')  156 us
    add x1024, other arithmetic, column_step(): upper = upper + jnp.where((places == step)[:, None], scaled[None, :], 0.0)  116 us
    dot_general x128, matrix products, row_step(): known = jnp.dot(beyond, inverse, precision=lax.Precision.HIGHEST)  91.1 us
    reduce_sum x128, other arithmetic, row_step(): diag_value = jnp.sum(jnp.where(places == index, row, 0.0))  76.8 us

commit v1 on v0

v1 whole, which is shorter than its diff:
```python
import functools

import jax
import jax.numpy as jnp
from jax import lax
from jax.experimental import pallas as pl
from jax.experimental.pallas import tpu as pltpu
from jax.sharding import PartitionSpec as P

MESH = pl.DeviceIdType.MESH
F32, BF16 = jnp.float32, jnp.bfloat16
NT = (((1,), (1,)), ((), ()))
TN = (((0,), (0,)), ((), ()))

D, K, ROWS = 4096, 128, 2816
HALF = D // 2
CHUNKS = (512, 512, 512, 512, 512, 256)
DEPTH = 2
SIZES = (768, 640, 640)
STARTS = (0, 768, 1408)
STRIDES = (2, 32, 8)
N_COPIES = 71


def split3(value):
    first = value.astype(BF16)
    rest = value - first.astype(F32)
    second = rest.astype(BF16)
    third = (rest - second.astype(F32)).astype(BF16)
    return first, second, third


def cholesky_blocks(remain, extra, inverse, low, high):
    sub = lax.broadcasted_iota(jnp.int32, (8, K), 0)

    def block_step(index, _):
        left, right = remain[0:8, :], extra[0:8, :]
        for j in range(8):
            column = jnp.broadcast_to(left[:, j : j + 1], (8, K))
            pivot = jnp.broadcast_to(column[j : j + 1, :], (8, K))
            scale = lax.rsqrt(pivot)
            scale = scale * (1.5 - 0.5 * pivot * scale * scale)
            left_row = jnp.broadcast_to(left[j : j + 1, :], (8, K)) * scale
            right_row = jnp.broadcast_to(right[j : j + 1, :], (8, K)) * scale
            factor = jnp.where(sub > j, column * scale, 0.0)
            left = jnp.where(sub == j, left_row, left - factor * left_row)
            right = jnp.where(sub == j, right_row, right - factor * right_row)
        inverse[pl.ds(pl.multiple_of(index * 8, 8), 8), :] = right
        both = jnp.concatenate([left, right], axis=1)
        one, two, three = (part.astype(F32) for part in split3(both))
        lhs = jnp.concatenate([one, one, two, two, one, three], axis=0)[:, :K].astype(BF16)
        rhs = jnp.concatenate([one, two, one, two, three, one], axis=0).astype(BF16)
        update = lax.dot_general(lhs, rhs, TN, preferred_element_type=F32)
        fresh = remain[...] - update[:, :K]
        remain[0 : K - 8, :] = pltpu.roll(fresh, K - 8, 1)[8:, :]
        remain[K - 8 :, :] = jnp.zeros((8, K), F32)
        extra[0 : K - 8, :] = extra[8:, :] - update[8:, K:]
        extra[K - 8 :, :] = jnp.zeros((8, K), F32)
        return 0

    lax.fori_loop(low, high, block_step, 0)


def main_kernel(
    a_hbm, s_hbm, o_hbm, w_ref,
    a, s, hl, outgo, income, half,
    r1a, r1b, r1c, s1a, s1b, s1c, r2a, r2b, r2c, r3a, r3b, r3c,
    whole, g_mine, g_core, g_one, g_two, g_three, g_full, g_extra, g_local,
    a_sem, s_sem, o_sem, send_sem, recv_sem,
):
    r1, s1, r2, r3 = (r1a, r1b, r1c), (s1a, s1b, s1c), (r2a, r2b, r2c), (r3a, r3b, r3c)
    me = lax.axis_index("tok")
    core = lax.rem(me, 2)
    partner = me + 1 - 2 * core
    place = [lax.rem(me // stride, 4) for stride in STRIDES]

    def at(axis, d):
        return lax.rem(place[axis] + d, 4)

    def device(axis, d):
        return me + (at(axis, d) - place[axis]) * STRIDES[axis]

    def rows(start, size):
        return pl.ds(pl.multiple_of(start, 8), size)

    starts = [sum(CHUNKS[:i]) for i in range(len(CHUNKS))]
    loads = [
        pltpu.make_async_copy(a_hbm.at[pl.ds(o, n)], a.at[pl.ds(o, n)], a_sem.at[i])
        for i, (o, n) in enumerate(zip(starts, CHUNKS))
    ]
    load_s = pltpu.make_async_copy(s_hbm, s, s_sem)
    load_s.start()
    for load in loads[:DEPTH]:
        load.start()

    barrier = pltpu.get_barrier_semaphore()
    pl.semaphore_signal(barrier, inc=1, device_id=(partner,), device_id_type=MESH)
    for axis in range(3):
        for d in (1, 2, 3):
            pl.semaphore_signal(barrier, inc=1, device_id=(device(axis, d),), device_id_type=MESH)

    sent = []

    def send(src, dst, target):
        i = len(sent)
        copy = pltpu.make_async_remote_copy(
            src_ref=src, dst_ref=dst, send_sem=send_sem.at[i], recv_sem=recv_sem.at[i],
            device_id=(target,), device_id_type=MESH,
        )
        copy.start()
        sent.append(copy)
        return copy

    load_s.wait()
    for i, (o, n) in enumerate(zip(starts, CHUNKS)):
        loads[i].wait()
        if i + DEPTH < len(loads):
            loads[i + DEPTH].start()
        sampled = jnp.dot(a[o : o + n, : D // 2], s[: D // 2, :], preferred_element_type=F32)
        sampled += jnp.dot(a[o : o + n, D // 2 :], s[D // 2 :, :], preferred_element_type=F32)
        turned = sampled.T
        high = turned.astype(BF16)
        hl[:K, o : o + n] = high
        hl[K:, o : o + n] = (turned - high.astype(F32)).astype(BF16)

    products = lax.dot_general(hl[...], hl[...], NT, preferred_element_type=F32)
    gram = (products[:K, :K] + products[K:, K:]) + (products[:K, K:] + products[K:, :K])
    g_local[...] = gram

    pl.semaphore_wait(barrier, 10)
    g_rows, g_other = rows(core * 64, 64), rows((1 - core) * 64, 64)
    g_copies = [send(g_local.at[g_other], g_core, partner)]

    def gram_stage(axis, slots, value):
        slots[place[axis]] = value
        mine = slots.at[place[axis]]
        return [send(mine, mine, device(axis, d)) for d in (1, 2, 3)]

    def gram_sum(copies, slots):
        for copy in copies:
            copy.wait_recv()
        return (slots[0] + slots[1]) + (slots[2] + slots[3])

    def columns(start, size):
        taken = a[:, pl.ds(pl.multiple_of(start, 128), size)]
        return jnp.dot(hl[:K, :], taken, preferred_element_type=F32).T

    to_core = []
    for j in range(3):
        piece = pl.ds(STARTS[j], SIZES[j])
        outgo[piece, :] = columns((1 - core) * HALF + STARTS[j], SIZES[j])
        to_core.append(send(outgo.at[piece], income.at[piece], partner))
        if j == 0:
            g_copies[0].wait_recv()
            g_copies = gram_stage(0, g_one, g_local[g_rows, :] + g_core[...])

    first = []
    for j in range(3):
        piece = pl.ds(STARTS[j], SIZES[j])
        quarter = SIZES[j] // 4
        value = columns(core * HALF + STARTS[j], SIZES[j])
        to_core[j].wait_recv()
        half[piece, :] = value + income[piece, :]
        first.append([
            send(half.at[rows(STARTS[j] + at(j, d) * quarter, quarter)], r1[j].at[d - 1], device(j, d))
            for d in (2, 1, 3)
        ])

    g_copies = gram_stage(1, g_two, gram_sum(g_copies, g_one))

    second = []
    for j in range(3):
        axis = (j + 1) % 3
        quarter, part = SIZES[j] // 4, SIZES[j] // 16
        for copy in first[j]:
            copy.wait_recv()
        s1[j][...] = (half[rows(STARTS[j] + place[j] * quarter, quarter), :] + r1[j][0]) + (r1[j][1] + r1[j][2])
        second.append([
            send(s1[j].at[rows(at(axis, d) * part, part)], r2[j].at[d - 1], device(axis, d))
            for d in (2, 1, 3)
        ])

    g_copies = gram_stage(2, g_three, gram_sum(g_copies, g_two))

    third = []
    for j in range(3):
        axis, last = (j + 1) % 3, (j + 2) % 3
        part = SIZES[j] // 16
        for copy in second[j]:
            copy.wait_recv()
        r3[j][place[last]] = (s1[j][rows(place[axis] * part, part), :] + r2[j][0]) + (r2[j][1] + r2[j][2])
        mine = r3[j].at[place[last]]
        third.append([send(mine, mine, device(last, d)) for d in (2, 1, 3)])

    g_mine[...] = gram_sum(g_copies, g_three)
    g_last = send(g_mine, g_full.at[g_rows], partner)
    g_full[g_rows, :] = g_mine[...]
    diagonal = lax.broadcasted_iota(jnp.int32, (K, K), 0) == lax.broadcasted_iota(jnp.int32, (K, K), 1)
    g_extra[...] = jnp.where(diagonal, 1.0, 0.0)
    g_last.wait_recv()
    cholesky_blocks(g_full, g_extra, w_ref, 0, 4)

    fourth = []
    for j in range(3):
        axis = (j + 1) % 3
        quarter, part = SIZES[j] // 4, SIZES[j] // 16
        for copy in third[j]:
            copy.wait_recv()
        here = rows(core * HALF + STARTS[j] + place[j] * quarter + place[axis] * part, part)
        whole[here, :] = (r3[j][0] + r3[j][1]) + (r3[j][2] + r3[j][3])
        fourth.append([send(whole.at[here], whole.at[here], device(axis, d)) for d in (2, 1, 3)])

    cholesky_blocks(g_full, g_extra, w_ref, 4, 10)

    fifth, forward = [], []
    for j in range(3):
        quarter = SIZES[j] // 4
        for copy in fourth[j]:
            copy.wait_recv()
        here = rows(core * HALF + STARTS[j] + place[j] * quarter, quarter)
        fifth.append([send(whole.at[here], whole.at[here], device(j, d)) for d in (2, 1, 3)])
        forward.append(send(whole.at[here], whole.at[here], partner))

    cholesky_blocks(g_full, g_extra, w_ref, 10, 16)

    for i, d in enumerate((2, 1, 3)):
        for j in (0, 1, 2):
            quarter = SIZES[j] // 4
            fifth[j][i].wait_recv()
            here = rows(core * HALF + STARTS[j] + at(j, 4 - d) * quarter, quarter)
            forward.append(send(whole.at[here], whole.at[here], partner))
    mine, other = rows(core * HALF, HALF), rows((1 - core) * HALF, HALF)
    out_mine = pltpu.make_async_copy(whole.at[mine], o_hbm.at[mine], o_sem.at[0])
    out_mine.start()
    for copy in forward:
        copy.wait_recv()
    out_other = pltpu.make_async_copy(whole.at[other], o_hbm.at[other], o_sem.at[1])
    out_other.start()
    for copy in sent:
        copy.wait_send()
    out_mine.wait()
    out_other.wait()


def apply_kernel(p_ref, w_ref, o_ref):
    p1, p2, p3 = split3(p_ref[...])
    w1, w2, w3 = (part.astype(F32).T.astype(BF16) for part in split3(w_ref[...]))
    wide = jnp.concatenate([w1, w2], axis=1)
    large = jnp.dot(
        jnp.concatenate([p1, p2], axis=1), jnp.concatenate([wide, wide], axis=0), preferred_element_type=F32
    )
    small = jnp.dot(
        jnp.concatenate([p1, p3], axis=1), jnp.concatenate([w3, w1], axis=0), preferred_element_type=F32
    )
    o_ref[...] = large[:, :K] + (large[:, K:] + small)


def local(activations, sketch):
    def slots(count, parts):
        return [pltpu.VMEM((count, size // parts, K), F32) for size in SIZES]

    partial, turned = pl.pallas_call(
        main_kernel,
        out_shape=[jax.ShapeDtypeStruct((D, K), F32), jax.ShapeDtypeStruct((K, K), F32)],
        in_specs=[pl.BlockSpec(memory_space=pl.ANY)] * 2,
        out_specs=[pl.BlockSpec(memory_space=pl.ANY), pl.BlockSpec(memory_space=pltpu.VMEM)],
        scratch_shapes=[
            pltpu.VMEM((ROWS, D), BF16),
            pltpu.VMEM((D, K), BF16),
            pltpu.VMEM((2 * K, ROWS), BF16),
            pltpu.VMEM((HALF, K), F32),
            pltpu.VMEM((HALF, K), F32),
            pltpu.VMEM((HALF, K), F32),
            *slots(3, 4),
            *[pltpu.VMEM((size // 4, K), F32) for size in SIZES],
            *slots(3, 16),
            *slots(4, 16),
            pltpu.VMEM((D, K), F32),
            pltpu.VMEM((64, K), F32),
            pltpu.VMEM((64, K), F32),
            pltpu.VMEM((4, 64, K), F32),
            pltpu.VMEM((4, 64, K), F32),
            pltpu.VMEM((4, 64, K), F32),
            pltpu.VMEM((K, K), F32),
            pltpu.VMEM((K, K), F32),
            pltpu.VMEM((K, K), F32),
            pltpu.SemaphoreType.DMA((len(CHUNKS),)),
            pltpu.SemaphoreType.DMA,
            pltpu.SemaphoreType.DMA((2,)),
            pltpu.SemaphoreType.DMA((N_COPIES,)),
            pltpu.SemaphoreType.DMA((N_COPIES,)),
        ],
        compiler_params=pltpu.CompilerParams(
            collective_id=0, has_side_effects=True, vmem_limit_bytes=48 * 2**20
        ),
    )(activations, sketch)
    tile = 1024
    return pl.pallas_call(
        apply_kernel,
        grid=(D // tile,),
        out_shape=jax.ShapeDtypeStruct((D, K), F32),
        in_specs=[pl.BlockSpec((tile, K), lambda i: (i, 0)), pl.BlockSpec((K, K), lambda i: (0, 0))],
        out_specs=pl.BlockSpec((tile, K), lambda i: (i, 0)),
        compiler_params=pltpu.CompilerParams(vmem_limit_bytes=32 * 2**20),
    )(partial, turned)


def solution(mesh):
    placed = (P("tok", None), P())
    return jax.shard_map(local, mesh=mesh, in_specs=placed, out_specs=P(), check_vma=False)
```

time: 2060 us -> 66.2 us (0.03)
  other arithmetic: 932 us -> 0 us
  loops' own time: 790 us -> 0 us
  waiting for transfers between devices: 165 us -> 0 us
  matrix products: 127 us -> 0 us
  Pallas kernels: 0 us -> 64.8 us
    another operation x9 -> x0, loops' own time: 790 us -> none  [the longest x8 785 us: upper_cholesky(): _, upper = lax.fori_loop(0, width, column_step, start)]
    reduce_sum x1152 -> x0, other arithmetic: 768 us -> none  [the longest x1024 692 us: column_step(): pivot = jnp.sqrt(jnp.sum(jnp.where(places == step, row, 0.0)))]
    psum x1 -> x0, waiting for transfers between devices: 156 us -> none  [local(): return lax.psum(term, 'tok')]
    add x1152 -> x0, other arithmetic: 127 us -> none  [the longest x1024 116 us: column_step(): upper = upper + jnp.where((places == step)[:, None], scaled[None, :], 0.0)]
    dot_general x146 -> x0, matrix products: 127 us -> none  [the longest x128 91.1 us: row_step(): known = jnp.dot(beyond, inverse, precision=lax.Precision.HIGHEST)]
    pallas_call x0 -> x2, Pallas kernels: none -> 64.8 us  [the longest x1 61.6 us: local(): pl.pallas_call(main_kernel, out_shape=[jax.ShapeDtypeStruct((D, K), F32),...]
where the time goes in v1:
time: 66.2 us; the launch traced here: 66.1 us
  Pallas kernels  64.8 us (98%)
  local copies, waits for them, and re-layouts  1.22 us (2%)
    pallas_call x1, Pallas kernels, local(): pl.pallas_call(main_kernel, out_shape=[jax.ShapeDtypeStruct((D, K), F32),...  61.6 us
    pallas_call x1, Pallas kernels, local(): pl.pallas_call(apply_kernel, grid=(D // tile,), out_shape=jax.ShapeDtypeS...  3.21 us

profile of v1, /device:TPU:1, one launch (start us, length us, event | category | flops | bytes accessed | tf_op | source)
XLA Modules:
  0.0 66.1 jit_solution(11250185151736799646)
XLA Ops:
  0.0 0.0 copy-start
  0.0 1.2 %copy-done = bf16[4096,128]{1,0:T(8,128)(2,1)S(1)} copy-done((bf16[4096,128]{1,0:T(8,128)(2,1)S(1)}, bf16[4096,128]{1,0:T(8,128)(2,1)}, u32[]{:S(2)}) %copy-start) | copy-done | bytes 1048600
  1.2 61.6 %shard_map.28 = (f32[4096,128]{1,0:T(8,128)S(1)}, f32[128,128]{1,0:T(8,128)S(1)}) custom-call(bf16[2816,4096]{1,0:T(8,128)(2,1)} %a_hbm.1, bf16[4096,128]{1,0:T(8,128)(2,1)S(1)} %copy-done), custom_call_target="tpu_custom_call" | custom-call | tf_op jit(solution)/shard_map/pallas_call | solution.py:262
  62.9 3.2 %shard_map.29 = f32[4096,128]{1,0:T(8,128)} custom-call(f32[4096,128]{1,0:T(8,128)S(1)} %get-tuple-element.7.p_ref, f32[128,128]{1,0:T(8,128)S(1)} %get-tuple-element.8.w_ref), custom_call_target="tpu_custom_call" | custom-call | tf_op jit(solution)/shard_map/pallas_call | solution.py:298
Async XLA Ops:
  0.0 1.2 %copy-start = (bf16[4096,128]{1,0:T(8,128)(2,1)S(1)}, bf16[4096,128]{1,0:T(8,128)(2,1)}, u32[]{:S(2)}) copy-start(bf16[4096,128]{1,0:T(8,128)(2,1)} %s_hbm.1) | copy-start | bytes 3145732

commit v2 on v1

--- a/solution.py
+++ b/solution.py
@@ -14,12 +14,13 @@
 
 D, K, ROWS = 4096, 128, 2816
 HALF = D // 2
-CHUNKS = (512, 512, 512, 512, 512, 256)
-DEPTH = 2
+CHUNKS = (256,) * 11
+DEPTH = 3
 SIZES = (768, 640, 640)
 STARTS = (0, 768, 1408)
 STRIDES = (2, 32, 8)
-N_COPIES = 71
+GRAM = ((0, 24), (24, 24), (48, 16))
+N_COPIES = 89
 
 
 def split3(value):
@@ -35,16 +36,29 @@
 
     def block_step(index, _):
         left, right = remain[0:8, :], extra[0:8, :]
+
+        def spread(value):
+            return jnp.broadcast_to(value, (8, K))
+
+        columns = [spread(left[:, j : j + 1]) for j in range(8)]
+        block = {(i, j): spread(columns[j][i : i + 1, :]) for j in range(8) for i in range(j, 8)}
+        lefts = [spread(left[i : i + 1, :]) for i in range(8)]
+        rights = [spread(right[i : i + 1, :]) for i in range(8)]
         for j in range(8):
-            column = jnp.broadcast_to(left[:, j : j + 1], (8, K))
-            pivot = jnp.broadcast_to(column[j : j + 1, :], (8, K))
+            pivot = block[j, j]
             scale = lax.rsqrt(pivot)
             scale = scale * (1.5 - 0.5 * pivot * scale * scale)
-            left_row = jnp.broadcast_to(left[j : j + 1, :], (8, K)) * scale
-            right_row = jnp.broadcast_to(right[j : j + 1, :], (8, K)) * scale
-            factor = jnp.where(sub > j, column * scale, 0.0)
-            left = jnp.where(sub == j, left_row, left - factor * left_row)
-            right = jnp.where(sub == j, right_row, right - factor * right_row)
+            factor = {i: block[i, j] * scale for i in range(j + 1, 8)}
+            lefts[j], rights[j] = lefts[j] * scale, rights[j] * scale
+            for i in range(j + 1, 8):
+                for k in range(j + 1, i + 1):
+                    block[i, k] = block[i, k] - factor[i] * factor[k]
+                lefts[i] = lefts[i] - factor[i] * lefts[j]
+                rights[i] = rights[i] - factor[i] * rights[j]
+        left, right = lefts[0], rights[0]
+        for j in range(1, 8):
+            left = jnp.where(sub == j, lefts[j], left)
+            right = jnp.where(sub == j, rights[j], right)
         inverse[pl.ds(pl.multiple_of(index * 8, 8), 8), :] = right
         both = jnp.concatenate([left, right], axis=1)
         one, two, three = (part.astype(F32) for part in split3(both))
@@ -62,11 +76,11 @@
 
 
 def main_kernel(
-    a_hbm, s_hbm, o_hbm, w_ref,
+    a_hbm, s_hbm, whole, w_ref,
     a, s, hl, outgo, income, half,
     r1a, r1b, r1c, s1a, s1b, s1c, r2a, r2b, r2c, r3a, r3b, r3c,
-    whole, g_mine, g_core, g_one, g_two, g_three, g_full, g_extra, g_local,
-    a_sem, s_sem, o_sem, send_sem, recv_sem,
+    g_mine, g_core, g_one, g_two, g_three, g_full, g_extra, g_local,
+    a_sem, s_sem, send_sem, recv_sem,
 ):
     r1, s1, r2, r3 = (r1a, r1b, r1c), (s1a, s1b, s1c), (r2a, r2b, r2c), (r3a, r3b, r3c)
     me = lax.axis_index("tok")
@@ -131,10 +145,14 @@
     g_rows, g_other = rows(core * 64, 64), rows((1 - core) * 64, 64)
     g_copies = [send(g_local.at[g_other], g_core, partner)]
 
-    def gram_stage(axis, slots, value):
-        slots[place[axis]] = value
-        mine = slots.at[place[axis]]
-        return [send(mine, mine, device(axis, d)) for d in (1, 2, 3)]
+    def gram_stage(stage, slots, value):
+        copies = []
+        for j, (start, size) in enumerate(GRAM):
+            axis = (j + stage) % 3
+            slots[place[axis], start : start + size, :] = value[start : start + size, :]
+            mine = slots.at[place[axis], pl.ds(start, size)]
+            copies += [send(mine, mine, device(axis, d)) for d in (2, 1, 3)]
+        return copies
 
     def gram_sum(copies, slots):
         for copy in copies:
@@ -197,8 +215,6 @@
     g_full[g_rows, :] = g_mine[...]
     diagonal = lax.broadcasted_iota(jnp.int32, (K, K), 0) == lax.broadcasted_iota(jnp.int32, (K, K), 1)
     g_extra[...] = jnp.where(diagonal, 1.0, 0.0)
-    g_last.wait_recv()
-    cholesky_blocks(g_full, g_extra, w_ref, 0, 4)
 
     fourth = []
     for j in range(3):
@@ -210,7 +226,8 @@
         whole[here, :] = (r3[j][0] + r3[j][1]) + (r3[j][2] + r3[j][3])
         fourth.append([send(whole.at[here], whole.at[here], device(axis, d)) for d in (2, 1, 3)])
 
-    cholesky_blocks(g_full, g_extra, w_ref, 4, 10)
+    g_last.wait_recv()
+    cholesky_blocks(g_full, g_extra, w_ref, 0, 7)
 
     fifth, forward = [], []
     for j in range(3):
@@ -221,7 +238,7 @@
         fifth.append([send(whole.at[here], whole.at[here], device(j, d)) for d in (2, 1, 3)])
         forward.append(send(whole.at[here], whole.at[here], partner))
 
-    cholesky_blocks(g_full, g_extra, w_ref, 10, 16)
+    cholesky_blocks(g_full, g_extra, w_ref, 7, 16)
 
     for i, d in enumerate((2, 1, 3)):
         for j in (0, 1, 2):
@@ -229,30 +246,28 @@
             fifth[j][i].wait_recv()
             here = rows(core * HALF + STARTS[j] + at(j, 4 - d) * quarter, quarter)
             forward.append(send(whole.at[here], whole.at[here], partner))
-    mine, other = rows(core * HALF, HALF), rows((1 - core) * HALF, HALF)
-    out_mine = pltpu.make_async_copy(whole.at[mine], o_hbm.at[mine], o_sem.at[0])
-    out_mine.start()
     for copy in forward:
         copy.wait_recv()
-    out_other = pltpu.make_async_copy(whole.at[other], o_hbm.at[other], o_sem.at[1])
-    out_other.start()
     for copy in sent:
         copy.wait_send()
-    out_mine.wait()
-    out_other.wait()
-
-
-def apply_kernel(p_ref, w_ref, o_ref):
-    p1, p2, p3 = split3(p_ref[...])
+
+
+def apply_kernel(tile, p_ref, w_ref, o_hbm, out, o_sem):
     w1, w2, w3 = (part.astype(F32).T.astype(BF16) for part in split3(w_ref[...]))
     wide = jnp.concatenate([w1, w2], axis=1)
-    large = jnp.dot(
-        jnp.concatenate([p1, p2], axis=1), jnp.concatenate([wide, wide], axis=0), preferred_element_type=F32
-    )
-    small = jnp.dot(
-        jnp.concatenate([p1, p3], axis=1), jnp.concatenate([w3, w1], axis=0), preferred_element_type=F32
-    )
-    o_ref[...] = large[:, :K] + (large[:, K:] + small)
+    large_w = jnp.concatenate([wide, wide], axis=0)
+    small_w = jnp.concatenate([w3, w1], axis=0)
+    copies = []
+    for i in range(D // tile):
+        piece = pl.ds(i * tile, tile)
+        p1, p2, p3 = split3(p_ref[piece, :])
+        large = jnp.dot(jnp.concatenate([p1, p2], axis=1), large_w, preferred_element_type=F32)
+        small = jnp.dot(jnp.concatenate([p1, p3], axis=1), small_w, preferred_element_type=F32)
+        out[piece, :] = large[:, :K] + (large[:, K:] + small)
+        copies.append(pltpu.make_async_copy(out.at[piece], o_hbm.at[piece], o_sem.at[i]))
+        copies[-1].start()
+    for copy in copies:
+        copy.wait()
 
 
 def local(activations, sketch):
@@ -262,8 +277,8 @@
     partial, turned = pl.pallas_call(
         main_kernel,
         out_shape=[jax.ShapeDtypeStruct((D, K), F32), jax.ShapeDtypeStruct((K, K), F32)],
-        in_specs=[pl.BlockSpec(memory_space=pl.ANY)] * 2,
-        out_specs=[pl.BlockSpec(memory_space=pl.ANY), pl.BlockSpec(memory_space=pltpu.VMEM)],
+        in_specs=[pl.BlockSpec(memory_space=pltpu.HBM)] * 2,
+        out_specs=[pl.BlockSpec(memory_space=pltpu.VMEM)] * 2,
         scratch_shapes=[
             pltpu.VMEM((ROWS, D), BF16),
             pltpu.VMEM((D, K), BF16),
@@ -275,7 +290,6 @@
             *[pltpu.VMEM((size // 4, K), F32) for size in SIZES],
             *slots(3, 16),
             *slots(4, 16),
-            pltpu.VMEM((D, K), F32),
             pltpu.VMEM((64, K), F32),
             pltpu.VMEM((64, K), F32),
             pltpu.VMEM((4, 64, K), F32),
@@ -286,7 +300,6 @@
             pltpu.VMEM((K, K), F32),
             pltpu.SemaphoreType.DMA((len(CHUNKS),)),
             pltpu.SemaphoreType.DMA,
-            pltpu.SemaphoreType.DMA((2,)),
             pltpu.SemaphoreType.DMA((N_COPIES,)),
             pltpu.SemaphoreType.DMA((N_COPIES,)),
         ],
@@ -294,13 +307,13 @@
             collective_id=0, has_side_effects=True, vmem_limit_bytes=48 * 2**20
         ),
     )(activations, sketch)
-    tile = 1024
+    tile = 512
     return pl.pallas_call(
-        apply_kernel,
-        grid=(D // tile,),
+        functools.partial(apply_kernel, tile),
         out_shape=jax.ShapeDtypeStruct((D, K), F32),
-        in_specs=[pl.BlockSpec((tile, K), lambda i: (i, 0)), pl.BlockSpec((K, K), lambda i: (0, 0))],
-        out_specs=pl.BlockSpec((tile, K), lambda i: (i, 0)),
+        in_specs=[pl.BlockSpec(memory_space=pltpu.VMEM)] * 2,
+        out_specs=pl.BlockSpec(memory_space=pltpu.HBM),
+        scratch_shapes=[pltpu.VMEM((D, K), F32), pltpu.SemaphoreType.DMA((D // tile,))],
         compiler_params=pltpu.CompilerParams(vmem_limit_bytes=32 * 2**20),
     )(partial, turned)
 

time: 66.2 us -> 52.4 us (0.79)
  Pallas kernels: 64.8 us -> 50.9 us
    pallas_call x1, Pallas kernels: 61.6 us -> 48.8 us  [local(): pl.pallas_call(main_kernel, out_shape=[jax.ShapeDtypeStruct((D, K), F32),...]
    pallas_call x1, Pallas kernels: 3.21 us -> 2.13 us  [local(): pl.pallas_call(functools.partial(apply_kernel, tile), out_shape=jax.Shape...]
where the time goes in v2:
time: 52.4 us; the launch traced here: 52.3 us
  Pallas kernels  50.9 us (97%)
  local copies, waits for them, and re-layouts  1.22 us (2%)
    pallas_call x1, Pallas kernels, local(): pl.pallas_call(main_kernel, out_shape=[jax.ShapeDtypeStruct((D, K), F32),...  48.8 us
    pallas_call x1, Pallas kernels, local(): pl.pallas_call(functools.partial(apply_kernel, tile), out_shape=jax.Shape...  2.13 us
    unnamed x2, local copies, waits for them, and re-layouts  1.22 us

profile of v2, /device:TPU:1, one launch (start us, length us, event | category | flops | bytes accessed | tf_op | source)
XLA Modules:
  0.0 52.3 jit_solution(7530106961191181023)
XLA Ops:
  0.0 0.0 copy-start
  0.0 1.2 %copy-done = bf16[4096,128]{1,0:T(8,128)(2,1)S(1)} copy-done((bf16[4096,128]{1,0:T(8,128)(2,1)S(1)}, bf16[4096,128]{1,0:T(8,128)(2,1)}, u32[]{:S(2)}) %copy-start) | copy-done | bytes 1048600
  1.2 48.8 %shard_map.28 = (f32[4096,128]{1,0:T(8,128)S(1)}, f32[128,128]{1,0:T(8,128)S(1)}) custom-call(bf16[2816,4096]{1,0:T(8,128)(2,1)} %a_hbm.1, bf16[4096,128]{1,0:T(8,128)(2,1)S(1)} %copy-done), custom_call_target="tpu_custom_call" | custom-call | tf_op jit(solution)/shard_map/pallas_call | solution.py:277
  50.0 2.1 %shard_map.29 = f32[4096,128]{1,0:T(8,128)} custom-call(f32[4096,128]{1,0:T(8,128)S(1)} %get-tuple-element.7.p_ref, f32[128,128]{1,0:T(8,128)S(1)} %get-tuple-element.8.w_ref), custom_call_target="tpu_custom_call" | custom-call | tf_op jit(solution)/shard_map/pallas_call | solution.py:311
Async XLA Ops:
  0.0 1.2 %copy-start = (bf16[4096,128]{1,0:T(8,128)(2,1)S(1)}, bf16[4096,128]{1,0:T(8,128)(2,1)}, u32[]{:S(2)}) copy-start(bf16[4096,128]{1,0:T(8,128)(2,1)} %s_hbm.1) | copy-start | bytes 3145732

commit v3 on v2

--- a/solution.py
+++ b/solution.py
@@ -16,8 +16,8 @@
 HALF = D // 2
 CHUNKS = (256,) * 11
 DEPTH = 3
-SIZES = (768, 640, 640)
-STARTS = (0, 768, 1408)
+SIZES = (768, 768, 512)
+STARTS = (0, 768, 1536)
 STRIDES = (2, 32, 8)
 GRAM = ((0, 24), (24, 24), (48, 16))
 N_COPIES = 89
@@ -76,11 +76,11 @@
 
 
 def main_kernel(
-    a_hbm, s_hbm, whole, w_ref,
-    a, s, hl, outgo, income, half,
+    a_hbm, s, whole, w_ref,
+    a, hl, outgo, income, half,
     r1a, r1b, r1c, s1a, s1b, s1c, r2a, r2b, r2c, r3a, r3b, r3c,
     g_mine, g_core, g_one, g_two, g_three, g_full, g_extra, g_local,
-    a_sem, s_sem, send_sem, recv_sem,
+    a_sem, send_sem, recv_sem,
 ):
     r1, s1, r2, r3 = (r1a, r1b, r1c), (s1a, s1b, s1c), (r2a, r2b, r2c), (r3a, r3b, r3c)
     me = lax.axis_index("tok")
@@ -102,8 +102,6 @@
         pltpu.make_async_copy(a_hbm.at[pl.ds(o, n)], a.at[pl.ds(o, n)], a_sem.at[i])
         for i, (o, n) in enumerate(zip(starts, CHUNKS))
     ]
-    load_s = pltpu.make_async_copy(s_hbm, s, s_sem)
-    load_s.start()
     for load in loads[:DEPTH]:
         load.start()
 
@@ -125,7 +123,6 @@
         sent.append(copy)
         return copy
 
-    load_s.wait()
     for i, (o, n) in enumerate(zip(starts, CHUNKS)):
         loads[i].wait()
         if i + DEPTH < len(loads):
@@ -163,17 +160,14 @@
         taken = a[:, pl.ds(pl.multiple_of(start, 128), size)]
         return jnp.dot(hl[:K, :], taken, preferred_element_type=F32).T
 
-    to_core = []
-    for j in range(3):
+    to_core, first = [], []
+
+    def theirs(j):
         piece = pl.ds(STARTS[j], SIZES[j])
         outgo[piece, :] = columns((1 - core) * HALF + STARTS[j], SIZES[j])
         to_core.append(send(outgo.at[piece], income.at[piece], partner))
-        if j == 0:
-            g_copies[0].wait_recv()
-            g_copies = gram_stage(0, g_one, g_local[g_rows, :] + g_core[...])
-
-    first = []
-    for j in range(3):
+
+    def ours(j):
         piece = pl.ds(STARTS[j], SIZES[j])
         quarter = SIZES[j] // 4
         value = columns(core * HALF + STARTS[j], SIZES[j])
@@ -184,6 +178,15 @@
             for d in (2, 1, 3)
         ])
 
+    theirs(0)
+    g_copies[0].wait_recv()
+    g_copies = gram_stage(0, g_one, g_local[g_rows, :] + g_core[...])
+    theirs(1)
+    ours(0)
+    theirs(2)
+    ours(1)
+    ours(2)
+
     g_copies = gram_stage(1, g_two, gram_sum(g_copies, g_one))
 
     second = []
@@ -227,8 +230,9 @@
         fourth.append([send(whole.at[here], whole.at[here], device(axis, d)) for d in (2, 1, 3)])
 
     g_last.wait_recv()
-    cholesky_blocks(g_full, g_extra, w_ref, 0, 7)
-
+    cholesky_blocks(g_full, g_extra, w_ref, 0, 8)
+
+    settled = len(sent)
     fifth, forward = [], []
     for j in range(3):
         quarter = SIZES[j] // 4
@@ -238,7 +242,9 @@
         fifth.append([send(whole.at[here], whole.at[here], device(j, d)) for d in (2, 1, 3)])
         forward.append(send(whole.at[here], whole.at[here], partner))
 
-    cholesky_blocks(g_full, g_extra, w_ref, 7, 16)
+    cholesky_blocks(g_full, g_extra, w_ref, 8, 16)
+    for copy in sent[:settled]:
+        copy.wait_send()
 
     for i, d in enumerate((2, 1, 3)):
         for j in (0, 1, 2):
@@ -248,7 +254,7 @@
             forward.append(send(whole.at[here], whole.at[here], partner))
     for copy in forward:
         copy.wait_recv()
-    for copy in sent:
+    for copy in sent[settled:]:
         copy.wait_send()
 
 
@@ -277,11 +283,10 @@
     partial, turned = pl.pallas_call(
         main_kernel,
         out_shape=[jax.ShapeDtypeStruct((D, K), F32), jax.ShapeDtypeStruct((K, K), F32)],
-        in_specs=[pl.BlockSpec(memory_space=pltpu.HBM)] * 2,
+        in_specs=[pl.BlockSpec(memory_space=pltpu.HBM), pl.BlockSpec(memory_space=pltpu.VMEM)],
         out_specs=[pl.BlockSpec(memory_space=pltpu.VMEM)] * 2,
         scratch_shapes=[
             pltpu.VMEM((ROWS, D), BF16),
-            pltpu.VMEM((D, K), BF16),
             pltpu.VMEM((2 * K, ROWS), BF16),
             pltpu.VMEM((HALF, K), F32),
             pltpu.VMEM((HALF, K), F32),
@@ -299,7 +304,6 @@
             pltpu.VMEM((K, K), F32),
             pltpu.VMEM((K, K), F32),
             pltpu.SemaphoreType.DMA((len(CHUNKS),)),
-            pltpu.SemaphoreType.DMA,
             pltpu.SemaphoreType.DMA((N_COPIES,)),
             pltpu.SemaphoreType.DMA((N_COPIES,)),
         ],

time: 52.4 us -> 52.6 us (level)
  no operation moved by 1% of the time
where the time goes in v3:
time: 52.6 us; the launch traced here: 52.5 us
  Pallas kernels  51.1 us (97%)
  local copies, waits for them, and re-layouts  1.22 us (2%)
    pallas_call x1, Pallas kernels, local(): pl.pallas_call(main_kernel, out_shape=[jax.ShapeDtypeStruct((D, K), F32),...  48.9 us
    pallas_call x1, Pallas kernels, local(): pl.pallas_call(functools.partial(apply_kernel, tile), out_shape=jax.Shape...  2.13 us
    unnamed x2, local copies, waits for them, and re-layouts  1.22 us

profile of v3, /device:TPU:1, one launch (start us, length us, event | category | flops | bytes accessed | tf_op | source)
XLA Modules:
  0.0 52.5 jit_solution(12558253379011327636)
XLA Ops:
  0.0 0.0 copy-start
  0.0 1.2 %copy-done = bf16[4096,128]{1,0:T(8,128)(2,1)S(1)} copy-done((bf16[4096,128]{1,0:T(8,128)(2,1)S(1)}, bf16[4096,128]{1,0:T(8,128)(2,1)}, u32[]{:S(2)}) %copy-start) | copy-done | bytes 1048600
  1.2 48.9 %shard_map.28 = (f32[4096,128]{1,0:T(8,128)S(1)}, f32[128,128]{1,0:T(8,128)S(1)}) custom-call(bf16[2816,4096]{1,0:T(8,128)(2,1)} %a_hbm.1, bf16[4096,128]{1,0:T(8,128)(2,1)S(1)} %copy-done), custom_call_target="tpu_custom_call" | custom-call | tf_op jit(solution)/shard_map/pallas_call | solution.py:283
  50.2 2.1 %shard_map.29 = f32[4096,128]{1,0:T(8,128)} custom-call(f32[4096,128]{1,0:T(8,128)S(1)} %get-tuple-element.7.p_ref, f32[128,128]{1,0:T(8,128)S(1)} %get-tuple-element.8.w_ref), custom_call_target="tpu_custom_call" | custom-call | tf_op jit(solution)/shard_map/pallas_call | solution.py:315
Async XLA Ops:
  0.0 1.2 %copy-start = (bf16[4096,128]{1,0:T(8,128)(2,1)S(1)}, bf16[4096,128]{1,0:T(8,128)(2,1)}, u32[]{:S(2)}) copy-start(bf16[4096,128]{1,0:T(8,128)(2,1)} %s.1) | copy-start | bytes 3145732

commit v4 on v3

--- a/solution.py
+++ b/solution.py
@@ -246,7 +246,7 @@
     for copy in sent[:settled]:
         copy.wait_send()
 
-    for i, d in enumerate((2, 1, 3)):
+    for i, d in ((1, 1), (2, 3), (0, 2)):
         for j in (0, 1, 2):
             quarter = SIZES[j] // 4
             fifth[j][i].wait_recv()

time: 52.6 us -> 53 us (level)
  no operation moved by 1% of the time
where the time goes in v4:
time: 53 us; the launch traced here: 52.8 us
  Pallas kernels  51.4 us (97%)
  local copies, waits for them, and re-layouts  1.22 us (2%)
    pallas_call x1, Pallas kernels, local(): pl.pallas_call(main_kernel, out_shape=[jax.ShapeDtypeStruct((D, K), F32),...  49.3 us
    pallas_call x1, Pallas kernels, local(): pl.pallas_call(functools.partial(apply_kernel, tile), out_shape=jax.Shape...  2.13 us
    unnamed x2, local copies, waits for them, and re-layouts  1.22 us

profile of v4, /device:TPU:1, one launch (start us, length us, event | category | flops | bytes accessed | tf_op | source)
XLA Modules:
  0.0 52.8 jit_solution(17209313901406565676)
XLA Ops:
  0.0 0.0 copy-start
  0.0 1.2 %copy-done = bf16[4096,128]{1,0:T(8,128)(2,1)S(1)} copy-done((bf16[4096,128]{1,0:T(8,128)(2,1)S(1)}, bf16[4096,128]{1,0:T(8,128)(2,1)}, u32[]{:S(2)}) %copy-start) | copy-done | bytes 1048600
  1.2 49.3 %shard_map.28 = (f32[4096,128]{1,0:T(8,128)S(1)}, f32[128,128]{1,0:T(8,128)S(1)}) custom-call(bf16[2816,4096]{1,0:T(8,128)(2,1)} %a_hbm.1, bf16[4096,128]{1,0:T(8,128)(2,1)S(1)} %copy-done), custom_call_target="tpu_custom_call" | custom-call | tf_op jit(solution)/shard_map/pallas_call | solution.py:283
  50.5 2.1 %shard_map.29 = f32[4096,128]{1,0:T(8,128)} custom-call(f32[4096,128]{1,0:T(8,128)S(1)} %get-tuple-element.7.p_ref, f32[128,128]{1,0:T(8,128)S(1)} %get-tuple-element.8.w_ref), custom_call_target="tpu_custom_call" | custom-call | tf_op jit(solution)/shard_map/pallas_call | solution.py:315
Async XLA Ops:
  0.0 1.2 %copy-start = (bf16[4096,128]{1,0:T(8,128)(2,1)S(1)}, bf16[4096,128]{1,0:T(8,128)(2,1)}, u32[]{:S(2)}) copy-start(bf16[4096,128]{1,0:T(8,128)(2,1)} %s.1) | copy-start | bytes 3145732
